TPU v7x, 32 devices: a whole 2x2x4 slice. The times are simulated.
32 devices in a mesh: row: 4 (over y, core), col: 8 (over z, x).
Axes of the slice: x: 2, y: 2, z: 4, core: 2. Of those that a mesh axis runs over, the one named last changes fastest.
Arguments:
- probes: bfloat16 [512, 16384], P(None, ('row', 'col')), may hold values from -6 to 6
- own_blocks: bfloat16 [3, 16384, 512], P(None, ('row', 'col')), may hold values from -0.1875 to 0.1875
- cross_blocks: bfloat16 [3, 16384, 512], P(None, ('row', 'col')), may hold values from -0.1875 to 0.1875
- level_perm: int32 [3, 16384], P(None, ('row', 'col')), may hold values from 0 to 511, as said below
Outputs:
- mixed: bfloat16 [512, 16384], P(None, ('row', 'col'))
Inputs may be any that keep to these rules, and one draw needn't show every extreme that they name: `level_perm`: each aligned run of 512 entries of a level is a permutation of 0 to 511.
All inputs are finite; a program needn't handle non-finite values.
Results may differ from a plain program's by a relative error of at most 0.0057.
Values may be sent and summed in bfloat16 or wider, within the bound.
A program may use at most 64 MiB of HBM per device.

v0:
```python
import jax
import jax.numpy as jnp
from jax import lax
from jax.sharding import PartitionSpec as P


def from_partner(value, axis, distance):
    mask = 2**distance
    pairs = [(source, source ^ mask) for source in range(lax.axis_size(axis))]
    return lax.ppermute(value, axis, pairs)


def combine(panel, partner, own, cross):
    total = jnp.dot(panel, own, preferred_element_type=jnp.float32)
    return total + jnp.dot(partner, cross, preferred_element_type=jnp.float32)


def across_col(panel, own, cross, bit):
    other = from_partner(panel, "col", bit)
    return combine(panel, other, own, cross)


def across_row(panel, own, cross, bit):
    other = from_partner(panel, "row", bit)
    return combine(panel, other, own, cross)


def per_device(probes, own_blocks, cross_blocks, level_perm):
    col_bits = lax.axis_size("col").bit_length() - 1
    row_bits = lax.axis_size("row").bit_length() - 1
    panel = probes
    for level in range(3):
        own = own_blocks[level]
        cross = cross_blocks[level]
        order = level_perm[level]
        if level == 0:
            total = across_col(panel, own, cross, col_bits - 1)
        elif level == 1:
            total = across_row(panel, own, cross, row_bits - 1)
        else:
            total = across_col(panel, own, cross, 0)
        total = jnp.take(total, order, axis=1)
        panel = total.astype(jnp.bfloat16)
    return panel


def solution(mesh):
    placed = (
        P(None, ("row", "col")),
        P(None, ("row", "col"), None),
        P(None, ("row", "col"), None),
        P(None, ("row", "col")),
    )
    return jax.shard_map(
        per_device, mesh=mesh, in_specs=placed, out_specs=P(None, ("row", "col")), check_vma=False
    )
```

profile of v0, /device:TPU:0, one launch (start us, length us, event | category | flops | bytes accessed | tf_op | source)
XLA Modules:
  0.0 62.4 jit_solution(9159554601930761872)
XLA Ops:
  0.0 0.0 copy-start
  0.0 4.0 %collective-permute-start = (bf16[512,512]{1,0:T(8,128)(2,1)}, bf16[512,512]{1,0:T(8,128)(2,1)S(1)}, u32[]{:S(2)}, u32[]{:S(2)}) collective-permute-start(bf16[512,512]{1,0:T(8,128)(2,1)} %param.6), channel_id=1, source_target_pairs={{0,4},{1,5},{2,6},{3,7},{4,0},{5,1},{6,2},{7,3},{8,12},{9,13},{10,... | collective-permute-start | bytes 1572872 | tf_op jit(solution)/shard_map/ppermute | solution.py:10
  4.0 0.8 %fusion.15 = (s32[1,512]{1,0:T(1,128)S(1)}, s32[1,512]{1,0:T(1,128)S(1)}, s32[1,512]{1,0:T(1,128)S(1)}) fusion(s32[3,512]{1,0:T(4,128)} %param.9), kind=kLoop, calls=%fused_computation.33 | loop fusion | bytes 12288 | tf_op jit(solution)/shard_map/slice | solution.py:35
  4.9 1.6 %fusion.7 = f32[512,512]{1,0:T(8,128)S(1)} fusion(bf16[512,512]{1,0:T(8,128)(2,1)} %param.6, bf16[3,512,512]{2,1,0:T(8,128)(2,1)} %param.7), kind=kOutput, calls=%fused_computation.16 | convolution fusion | flops 268435456 | bytes 2097152 | tf_op jit(solution)/shard_map/dot_general | solution.py:14
  6.6 20.9 %collective-permute-done = bf16[512,512]{1,0:T(8,128)(2,1)S(1)} collective-permute-done((bf16[512,512]{1,0:T(8,128)(2,1)}, bf16[512,512]{1,0:T(8,128)(2,1)S(1)}, u32[]{:S(2)}, u32[]{:S(2)}) %collective-permute-start) | collective-permute-done | bytes 524320 | tf_op jit(solution)/shard_map/ppermute | solution.py:10
  27.4 0.0 copy-done
  27.4 0.4 convolution_add_fusion.2
  27.8 0.2 copy.5
  28.1 2.0 %gather_fusion = bf16[512,512]{1,0:T(8,128)(2,1)S(1)} fusion(bf16[512,512]{0,1:T(8,128)(2,1)S(1)} %copy.5, s32[1024]{0:T(1024)S(1)} %pad_clamp_fusion.2), kind=kCustom, calls=%fused_computation.clone | custom fusion | bytes 1050624 | tf_op jit(solution)/shard_map/jit(_take)/gather | solution.py:42
  30.0 0.2 bitcast_convert_fusion.2
  30.2 1.6 %collective-permute-start.1 = (bf16[512,512]{0,1:T(8,128)(2,1)S(1)}, bf16[512,512]{0,1:T(8,128)(2,1)S(1)}, u32[]{:S(2)}, u32[]{:S(2)}) collective-permute-start(bf16[512,512]{0,1:T(8,128)(2,1)S(1)} %bitcast_convert_fusion.2), channel_id=1, source_target_pairs={{0,16},{8,24},{16,0},{24,8},{1,17},{9,25},{17,1},{25,9},{2,18},{10... | collective-permute-start | bytes 1572872 | tf_op jit(solution)/shard_map/ppermute | solution.py:10
  31.9 1.5 %fusion.4 = f32[512,512]{1,0:T(8,128)S(1)} fusion(bf16[512,512]{0,1:T(8,128)(2,1)S(1)} %bitcast_convert_fusion.2, bf16[3,512,512]{2,1,0:T(8,128)(2,1)} %param.7), kind=kOutput, calls=%fused_computation.13 | convolution fusion | flops 268435456 | bytes 2097152 | tf_op jit(solution)/shard_map/dot_general | solution.py:14
  33.4 10.0 %collective-permute-done.1 = bf16[512,512]{0,1:T(8,128)(2,1)S(1)} collective-permute-done((bf16[512,512]{0,1:T(8,128)(2,1)S(1)}, bf16[512,512]{0,1:T(8,128)(2,1)S(1)}, u32[]{:S(2)}, u32[]{:S(2)}) %collective-permute-start.1) | collective-permute-done | bytes 524320 | tf_op jit(solution)/shard_map/ppermute | solution.py:10
  43.4 0.5 convolution_add_fusion.1
  43.9 0.2 copy.6
  44.1 2.0 %gather_fusion.1 = bf16[512,512]{1,0:T(8,128)(2,1)S(1)} fusion(bf16[512,512]{0,1:T(8,128)(2,1)S(1)} %copy.6, s32[1024]{0:T(1024)S(1)} %pad_clamp_fusion.1), kind=kCustom, calls=%fused_computation.1.clone | custom fusion | bytes 1050624 | tf_op jit(solution)/shard_map/jit(_take)/gather | solution.py:42
  46.1 0.2 bitcast_convert_fusion.1
  46.3 1.3 %collective-permute-start.2 = (bf16[512,512]{0,1:T(8,128)(2,1)S(1)}, bf16[512,512]{0,1:T(8,128)(2,1)S(1)}, u32[]{:S(2)}, u32[]{:S(2)}) collective-permute-start(bf16[512,512]{0,1:T(8,128)(2,1)S(1)} %bitcast_convert_fusion.1), channel_id=1, source_target_pairs={{0,1},{1,0},{2,3},{3,2},{4,5},{5,4},{6,7},{7,6},{8,9},{9,8},{10,11... | collective-permute-start | bytes 1572872 | tf_op jit(solution)/shard_map/ppermute | solution.py:10
  47.6 1.5 %fusion.1 = f32[512,512]{1,0:T(8,128)S(1)} fusion(bf16[512,512]{0,1:T(8,128)(2,1)S(1)} %bitcast_convert_fusion.1, bf16[3,512,512]{2,1,0:T(8,128)(2,1)} %param.7), kind=kOutput, calls=%fused_computation.10 | convolution fusion | flops 268435456 | bytes 2097152 | tf_op jit(solution)/shard_map/dot_general | solution.py:14
  49.1 9.4 %collective-permute-done.2 = bf16[512,512]{0,1:T(8,128)(2,1)S(1)} collective-permute-done((bf16[512,512]{0,1:T(8,128)(2,1)S(1)}, bf16[512,512]{0,1:T(8,128)(2,1)S(1)}, u32[]{:S(2)}, u32[]{:S(2)}) %collective-permute-start.2) | collective-permute-done | bytes 524320 | tf_op jit(solution)/shard_map/ppermute | solution.py:10
  58.5 0.5 convolution_add_fusion
  59.0 0.2 copy.7
  59.2 2.0 %gather_fusion.2 = bf16[512,512]{1,0:T(8,128)(2,1)S(1)} fusion(bf16[512,512]{0,1:T(8,128)(2,1)S(1)} %copy.7, s32[1024]{0:T(1024)S(1)} %pad_clamp_fusion), kind=kCustom, calls=%fused_computation.2.clone | custom fusion | bytes 1050624 | tf_op jit(solution)/shard_map/jit(_take)/gather | solution.py:42
  61.2 0.2 bitcast_convert_fusion
  61.4 1.0 %copy.8 = bf16[512,512]{1,0:T(8,128)(2,1)} copy(bf16[512,512]{0,1:T(8,128)(2,1)S(1)} %bitcast_convert_fusion) | data formatting | bytes 1048576 | tf_op jit(solution)/shard_map/convert_element_type | solution.py:43
  (9 shorter events, 0.1 us)
Async XLA Ops:
  0.0 27.4 %copy-start = (bf16[3,512,512]{2,1,0:T(8,128)(2,1)S(1)}, bf16[3,512,512]{2,1,0:T(8,128)(2,1)}, u32[]{:S(2)}) copy-start(bf16[3,512,512]{2,1,0:T(8,128)(2,1)} %param.8) | copy-start | bytes 4718596
  0.0 27.4 %collective-permute-start = (bf16[512,512]{1,0:T(8,128)(2,1)}, bf16[512,512]{1,0:T(8,128)(2,1)S(1)}, u32[]{:S(2)}, u32[]{:S(2)}) collective-permute-start(bf16[512,512]{1,0:T(8,128)(2,1)} %param.6), channel_id=1, source_target_pairs={{0,4},{1,5},{2,6},{3,7},{4,0},{5,1},{6,2},{7,3},{8,12},{9,13},{10,... | collective-permute-start | bytes 1572872 | tf_op jit(solution)/shard_map/ppermute | solution.py:10
  30.2 13.2 %collective-permute-start.1 = (bf16[512,512]{0,1:T(8,128)(2,1)S(1)}, bf16[512,512]{0,1:T(8,128)(2,1)S(1)}, u32[]{:S(2)}, u32[]{:S(2)}) collective-permute-start(bf16[512,512]{0,1:T(8,128)(2,1)S(1)} %bitcast_convert_fusion.2), channel_id=1, source_target_pairs={{0,16},{8,24},{16,0},{24,8},{1,17},{9,25},{17,1},{25,9},{2,18},{10... | collective-permute-start | bytes 1572872 | tf_op jit(solution)/shard_map/ppermute | solution.py:10
  46.3 12.3 %collective-permute-start.2 = (bf16[512,512]{0,1:T(8,128)(2,1)S(1)}, bf16[512,512]{0,1:T(8,128)(2,1)S(1)}, u32[]{:S(2)}, u32[]{:S(2)}) collective-permute-start(bf16[512,512]{0,1:T(8,128)(2,1)S(1)} %bitcast_convert_fusion.1), channel_id=1, source_target_pairs={{0,1},{1,0},{2,3},{3,2},{4,5},{5,4},{6,7},{7,6},{8,9},{9,8},{10,11... | collective-permute-start | bytes 1572872 | tf_op jit(solution)/shard_map/ppermute | solution.py:10
where the time goes:
time: 62.7 us; the launch traced here: 62.4 us
  waiting for transfers between devices  40.3 us (64%)
  local copies, waits for them, and re-layouts  8.38 us (13%)
  starting transfers between devices  6.99 us (11%)
  matrix products  6.01 us (10%)
    ppermute x3, waiting for transfers between devices, from_partner(): return lax.ppermute(value, axis, pairs)  40.3 us
    ppermute x3, starting transfers between devices, from_partner(): return lax.ppermute(value, axis, pairs)  6.99 us
    gather x3, local copies, waits for them, and re-layouts, per_device(): total = jnp.take(total, order, axis=1)  5.91 us
    dot_general x3, matrix products, combine(): total = jnp.dot(panel, own, preferred_element_type=jnp.float32)  4.65 us
    dot_general x3, matrix products, combine(): return total + jnp.dot(partner, cross, preferred_element_type=jnp.float32)  1.36 us
  transfers between devices with their start and end apart: 3, of which 3 were waited for; matrix products, arithmetic and copies ran while one was open for 9% of the time, Pallas kernels for 0%

commit v1 on v0

v1 whole, which is shorter than its diff:
```python
import functools

import jax
import jax.numpy as jnp
from jax import lax
from jax.experimental import pallas as pl
from jax.experimental.pallas import tpu as pltpu
from jax.sharding import PartitionSpec as P

LEVELS = 3
BODY = 64
TAIL = (48, 32, 32, 16)


def row_chunks(rows):
    sizes = list(TAIL) if rows > sum(TAIL) else []
    left = rows - sum(sizes)
    head = [BODY] * (left // BODY)
    if left % BODY:
        head.append(left % BODY)
    chunks, start = [], 0
    for size in head + sizes:
        chunks.append((start, size))
        start += size
    return chunks


def flip(index, distance):
    return index + distance - 2 * distance * lax.rem(lax.div(index, distance), 2)


def kernel(
    n_row, n_col, chunks,
    probes, own, cross, perm,
    out,
    mine, own_v, cross_v, perm_v, own_p, cross_p, panels, others,
    load_sem, perm_sem, send_sem, recv_sem,
):
    row, col = lax.axis_index("row"), lax.axis_index("col")
    partners = [
        (row, flip(col, n_col // 2)),
        (flip(row, n_row // 2), col),
        (row, flip(col, 1)),
    ]
    barrier = pltpu.get_barrier_semaphore()
    for partner in partners:
        pl.semaphore_signal(
            barrier, inc=1, device_id=partner, device_id_type=pl.DeviceIdType.MESH
        )
    loads = [
        pltpu.make_async_copy(perm, perm_v, perm_sem),
        pltpu.make_async_copy(own, own_v, load_sem.at[0]),
        pltpu.make_async_copy(cross, cross_v, load_sem.at[1]),
        pltpu.make_async_copy(probes, mine, load_sem.at[2]),
    ]
    for load in loads:
        load.start()
    pl.semaphore_wait(barrier, LEVELS)

    def send(level, k):
        start, size = chunks[k]
        rows = pl.ds(start, size)
        source = probes.at[rows] if level == 0 else panels.at[level - 1, rows]
        return pltpu.make_async_remote_copy(
            src_ref=source,
            dst_ref=others.at[level, rows],
            send_sem=send_sem.at[level, k],
            recv_sem=recv_sem.at[level, k],
            device_id=partners[level],
            device_id_type=pl.DeviceIdType.MESH,
        )

    copies = {}
    for k in range(len(chunks)):
        copies[0, k] = send(0, k)
        copies[0, k].start()

    for load in loads:
        load.wait()
    depth = own.shape[1]
    for level in range(LEVELS):
        index = lax.broadcasted_iota(jnp.int32, (depth, depth), 0)
        pick = jnp.where(index == perm_v[level : level + 1, :], 1.0, 0.0).astype(jnp.bfloat16)
        for source, target in ((own_v, own_p), (cross_v, cross_p)):
            moved = jnp.dot(source[level], pick, preferred_element_type=jnp.float32)
            target[level] = moved.astype(jnp.bfloat16)

    def step(level, k):
        start, size = chunks[k]
        rows = pl.ds(start, size)
        held = mine[rows] if level == 0 else panels[level - 1, rows]
        total = jnp.dot(held, own_p[level], preferred_element_type=jnp.float32)
        copies[level, k].wait_recv()
        total += jnp.dot(others[level, rows], cross_p[level], preferred_element_type=jnp.float32)
        result = total.astype(jnp.bfloat16)
        if level < LEVELS - 1:
            panels[level, rows] = result
            copies[level + 1, k] = send(level + 1, k)
            copies[level + 1, k].start()
        else:
            out[rows] = result

    for k in range(len(chunks) + LEVELS - 1):
        for level in range(LEVELS):
            if 0 <= k - level < len(chunks):
                step(level, k - level)
    for copy in copies.values():
        copy.wait_send()


def per_device(n_row, n_col, probes, own_blocks, cross_blocks, level_perm):
    rows, depth = probes.shape
    chunks = row_chunks(rows)
    weights = pltpu.VMEM(own_blocks.shape, jnp.bfloat16)
    return pl.pallas_call(
        functools.partial(kernel, n_row, n_col, chunks),
        out_shape=jax.ShapeDtypeStruct((rows, depth), jnp.bfloat16),
        in_specs=[pl.BlockSpec(memory_space=pltpu.HBM)] * 4,
        out_specs=pl.BlockSpec(memory_space=pltpu.VMEM),
        scratch_shapes=[
            pltpu.VMEM((rows, depth), jnp.bfloat16),
            weights,
            weights,
            pltpu.VMEM(level_perm.shape, jnp.int32),
            weights,
            weights,
            pltpu.VMEM((LEVELS - 1, rows, depth), jnp.bfloat16),
            pltpu.VMEM((LEVELS, rows, depth), jnp.bfloat16),
            pltpu.SemaphoreType.DMA((3,)),
            pltpu.SemaphoreType.DMA,
            pltpu.SemaphoreType.DMA((LEVELS, len(chunks))),
            pltpu.SemaphoreType.DMA((LEVELS, len(chunks))),
        ],
        compiler_params=pltpu.CompilerParams(
            collective_id=0, has_side_effects=True, vmem_limit_bytes=60 * 2**20
        ),
        cost_estimate=pl.CostEstimate(
            flops=24 * rows * depth * depth, bytes_accessed=8 * rows * depth * 2, transcendentals=0
        ),
    )(probes, own_blocks, cross_blocks, level_perm)


def solution(mesh):
    n_row, n_col = mesh.shape["row"], mesh.shape["col"]
    placed = (
        P(None, ("row", "col")),
        P(None, ("row", "col"), None),
        P(None, ("row", "col"), None),
        P(None, ("row", "col")),
    )
    return jax.shard_map(
        functools.partial(per_device, n_row, n_col),
        mesh=mesh,
        in_specs=placed,
        out_specs=P(None, ("row", "col")),
        check_vma=False,
    )
```

time: 62.7 us -> 52.9 us (0.84)
  Pallas kernels: 0 us -> 50.9 us
  waiting for transfers between devices: 40.3 us -> 0 us
  starting transfers between devices: 6.99 us -> 0 us
  local copies, waits for them, and re-layouts: 8.38 us -> 1.87 us
  matrix products: 6.01 us -> 0 us
    pallas_call x0 -> x1, Pallas kernels: none -> 50.9 us  [per_device(): pl.pallas_call(functools.partial(kernel, n_row, n_col, chunks), out_shape...]
    ppermute x3 -> x0, waiting for transfers between devices: 40.3 us -> none  [from_partner(): return lax.ppermute(value, axis, pairs)]
    ppermute x3 -> x0, starting transfers between devices: 6.99 us -> none  [from_partner(): return lax.ppermute(value, axis, pairs)]
    dot_general x6 -> x0, matrix products: 6.01 us -> none  [the longest x3 4.65 us: combine(): total = jnp.dot(panel, own, preferred_element_type=jnp.float32)]
    gather x3 -> x0, local copies, waits for them, and re-layouts: 5.91 us -> none  [per_device(): total = jnp.take(total, order, axis=1)]
    unnamed x2 -> x1, local copies, waits for them, and re-layouts: 0.01 us -> 1.87 us
    convert_element_type x1 -> x0, local copies, waits for them, and re-layouts: 1 us -> none  [per_device(): panel = total.astype(jnp.bfloat16)]
    slice x1 -> x0, local copies, waits for them, and re-layouts: 0.81 us -> none  [per_device(): order = level_perm[level]]
  transfers between devices with their start and end apart: 3 -> 0, of which waited for: 3 -> 0; matrix products, arithmetic and copies ran while one was open for 9% -> 0% of each run, Pallas kernels for 0% -> 0%
where the time goes in v1:
time: 52.9 us; the launch traced here: 52.8 us
  Pallas kernels  50.9 us (96%)
  local copies, waits for them, and re-layouts  1.87 us (4%)
    pallas_call x1, Pallas kernels, per_device(): pl.pallas_call(functools.partial(kernel, n_row, n_col, chunks), out_shape...  50.9 us
    unnamed x1, local copies, waits for them, and re-layouts  1.87 us

profile of v1, /device:TPU:0, one launch (start us, length us, event | category | flops | bytes accessed | tf_op | source)
XLA Modules:
  0.0 52.8 jit_solution(13793428892307918146)
XLA Ops:
  0.0 50.9 %shard_map.46 = bf16[512,512]{1,0:T(8,128)(2,1)} custom-call(bf16[512,512]{1,0:T(8,128)(2,1)} %probes.1, bf16[3,512,512]{2,1,0:T(8,128)(2,1)} %own.1, bf16[3,512,512]{2,1,0:T(8,128)(2,1)} %cross.1, s32[3,512]{1,0:T(4,128)} %perm.1), custom_call_target="tpu_custom_call" | custom-call | flops 3221225472 | bytes 4194304 | tf_op jit(solution)/shard_map/pallas_call | solution.py:115
  50.9 1.9 %copy.6 = bf16[512,512]{1,0:T(8,128)(2,1)} copy(bf16[512,512]{1,0:T(8,128)(2,1)} %shard_map.46) | data formatting | bytes 1048576

commit v2 on v1

--- a/solution.py
+++ b/solution.py
@@ -8,8 +8,9 @@
 from jax.sharding import PartitionSpec as P
 
 LEVELS = 3
-BODY = 64
-TAIL = (48, 32, 32, 16)
+BODY = 32
+TAIL = (16, 16)
+AHEAD = 3
 
 
 def row_chunks(rows):
@@ -71,7 +72,7 @@
         )
 
     copies = {}
-    for k in range(len(chunks)):
+    for k in range(min(AHEAD, len(chunks))):
         copies[0, k] = send(0, k)
         copies[0, k].start()
 
@@ -91,6 +92,9 @@
         held = mine[rows] if level == 0 else panels[level - 1, rows]
         total = jnp.dot(held, own_p[level], preferred_element_type=jnp.float32)
         copies[level, k].wait_recv()
+        if level == 0 and k + AHEAD < len(chunks):
+            copies[0, k + AHEAD] = send(0, k + AHEAD)
+            copies[0, k + AHEAD].start()
         total += jnp.dot(others[level, rows], cross_p[level], preferred_element_type=jnp.float32)
         result = total.astype(jnp.bfloat16)
         if level < LEVELS - 1:

time: 52.9 us -> 54.9 us (1.038)
  Pallas kernels: 50.9 us -> 52.8 us
    pallas_call x1, Pallas kernels: 50.9 us -> 52.8 us  [per_device(): pl.pallas_call(functools.partial(kernel, n_row, n_col, chunks), out_shape...]
where the time goes in v2:
time: 54.9 us; the launch traced here: 54.7 us
  Pallas kernels  52.8 us (96%)
  local copies, waits for them, and re-layouts  1.87 us (3%)
    pallas_call x1, Pallas kernels, per_device(): pl.pallas_call(functools.partial(kernel, n_row, n_col, chunks), out_shape...  52.8 us
    unnamed x1, local copies, waits for them, and re-layouts  1.87 us

profile of v2, /device:TPU:0, one launch (start us, length us, event | category | flops | bytes accessed | tf_op | source)
XLA Modules:
  0.0 54.7 jit_solution(11371228161198224633)
XLA Ops:
  0.0 52.8 %shard_map.46 = bf16[512,512]{1,0:T(8,128)(2,1)} custom-call(bf16[512,512]{1,0:T(8,128)(2,1)} %probes.1, bf16[3,512,512]{2,1,0:T(8,128)(2,1)} %own.1, bf16[3,512,512]{2,1,0:T(8,128)(2,1)} %cross.1, s32[3,512]{1,0:T(4,128)} %perm.1), custom_call_target="tpu_custom_call" | custom-call | flops 3221225472 | bytes 4194304 | tf_op jit(solution)/shard_map/pallas_call | solution.py:119
  52.8 1.9 %copy.6 = bf16[512,512]{1,0:T(8,128)(2,1)} copy(bf16[512,512]{1,0:T(8,128)(2,1)} %shard_map.46) | data formatting | bytes 1048576

commit v3 on v2

--- a/solution.py
+++ b/solution.py
@@ -10,7 +10,8 @@
 LEVELS = 3
 BODY = 32
 TAIL = (16, 16)
-AHEAD = 3
+AHEAD = 4
+LAG = 96
 
 
 def row_chunks(rows):
@@ -24,6 +25,11 @@
         chunks.append((start, size))
         start += size
     return chunks
+
+
+def step_order(chunks):
+    steps = [(level, k) for k in range(len(chunks)) for level in range(LEVELS)]
+    return sorted(steps, key=lambda s: (sum(chunks[s[1]]) + s[0] * LAG, s[0]))
 
 
 def flip(index, distance):
@@ -104,10 +110,8 @@
         else:
             out[rows] = result
 
-    for k in range(len(chunks) + LEVELS - 1):
-        for level in range(LEVELS):
-            if 0 <= k - level < len(chunks):
-                step(level, k - level)
+    for level, k in step_order(chunks):
+        step(level, k)
     for copy in copies.values():
         copy.wait_send()
 

time: 54.9 us -> 39.6 us (0.72)
  the two profiles are of different devices: /device:TPU:0 before, /device:TPU:10 now
where the time goes in v3:
time: 39.6 us; the launch traced here: 39.5 us
  Pallas kernels  37.6 us (95%)
  local copies, waits for them, and re-layouts  1.87 us (5%)
    pallas_call x1, Pallas kernels, per_device(): pl.pallas_call(functools.partial(kernel, n_row, n_col, chunks), out_shape...  37.6 us
    unnamed x1, local copies, waits for them, and re-layouts  1.87 us

profile of v3, /device:TPU:10, one launch (start us, length us, event | category | flops | bytes accessed | tf_op | source)
XLA Modules:
  0.0 39.5 jit_solution(17440381619220032526)
XLA Ops:
  0.0 37.6 %shard_map.46 = bf16[512,512]{1,0:T(8,128)(2,1)} custom-call(bf16[512,512]{1,0:T(8,128)(2,1)} %probes.1, bf16[3,512,512]{2,1,0:T(8,128)(2,1)} %own.1, bf16[3,512,512]{2,1,0:T(8,128)(2,1)} %cross.1, s32[3,512]{1,0:T(4,128)} %perm.1), custom_call_target="tpu_custom_call" | custom-call | flops 3221225472 | bytes 4194304 | tf_op jit(solution)/shard_map/pallas_call | solution.py:123
  37.6 1.9 %copy.6 = bf16[512,512]{1,0:T(8,128)(2,1)} copy(bf16[512,512]{1,0:T(8,128)(2,1)} %shard_map.46) | data formatting | bytes 1048576

commit v4 on v3

--- a/solution.py
+++ b/solution.py
@@ -11,7 +11,7 @@
 BODY = 32
 TAIL = (16, 16)
 AHEAD = 4
-LAG = 96
+LAG = 32
 
 
 def row_chunks(rows):
@@ -28,8 +28,14 @@
 
 
 def step_order(chunks):
-    steps = [(level, k) for k in range(len(chunks)) for level in range(LEVELS)]
-    return sorted(steps, key=lambda s: (sum(chunks[s[1]]) + s[0] * LAG, s[0]))
+    rows = sum(chunks[-1])
+    steps = []
+    for k, chunk in enumerate(chunks):
+        due = sum(chunk)
+        for level in range(LEVELS):
+            steps.append((due, level, k))
+            due += min((AHEAD - 1) * BODY, max(rows - due, 0)) + LAG
+    return [(level, k) for _, level, k in sorted(steps)]
 
 
 def flip(index, distance):
@@ -98,15 +104,15 @@
         held = mine[rows] if level == 0 else panels[level - 1, rows]
         total = jnp.dot(held, own_p[level], preferred_element_type=jnp.float32)
         copies[level, k].wait_recv()
-        if level == 0 and k + AHEAD < len(chunks):
-            copies[0, k + AHEAD] = send(0, k + AHEAD)
-            copies[0, k + AHEAD].start()
         total += jnp.dot(others[level, rows], cross_p[level], preferred_element_type=jnp.float32)
         result = total.astype(jnp.bfloat16)
         if level < LEVELS - 1:
             panels[level, rows] = result
             copies[level + 1, k] = send(level + 1, k)
             copies[level + 1, k].start()
+        if level == 0 and k + AHEAD < len(chunks):
+            copies[0, k + AHEAD] = send(0, k + AHEAD)
+            copies[0, k + AHEAD].start()
         else:
             out[rows] = result
 
@@ -120,6 +126,10 @@
     rows, depth = probes.shape
     chunks = row_chunks(rows)
     weights = pltpu.VMEM(own_blocks.shape, jnp.bfloat16)
+    probes, own_blocks, cross_blocks, level_perm = (
+        pltpu.with_memory_space_constraint(a, pltpu.HBM)
+        for a in (probes, own_blocks, cross_blocks, level_perm)
+    )
     return pl.pallas_call(
         functools.partial(kernel, n_row, n_col, chunks),
         out_shape=jax.ShapeDtypeStruct((rows, depth), jnp.bfloat16),
@@ -140,7 +150,7 @@
             pltpu.SemaphoreType.DMA((LEVELS, len(chunks))),
         ],
         compiler_params=pltpu.CompilerParams(
-            collective_id=0, has_side_effects=True, vmem_limit_bytes=60 * 2**20
+            collective_id=0, has_side_effects=True, vmem_limit_bytes=32 * 2**20
         ),
         cost_estimate=pl.CostEstimate(
             flops=24 * rows * depth * depth, bytes_accessed=8 * rows * depth * 2, transcendentals=0

time: 39.6 us -> 37.8 us (0.955)
  the two profiles are of different devices: /device:TPU:10 before, /device:TPU:8 now
where the time goes in v4:
time: 37.8 us; the launch traced here: 37.7 us
  Pallas kernels  36.9 us (98%)
  local copies, waits for them, and re-layouts  0.8 us (2%)
    pallas_call x1, Pallas kernels, per_device(): pl.pallas_call(functools.partial(kernel, n_row, n_col, chunks), out_shape...  36.9 us
    unnamed x1, local copies, waits for them, and re-layouts  0.8 us

profile of v4, /device:TPU:8, one launch (start us, length us, event | category | flops | bytes accessed | tf_op | source)
XLA Modules:
  0.0 37.7 jit_solution(7489319532081817494)
XLA Ops:
  0.0 36.9 %shard_map.46 = bf16[512,512]{1,0:T(8,128)(2,1)S(1)} custom-call(bf16[512,512]{1,0:T(8,128)(2,1)} %probes.1, bf16[3,512,512]{2,1,0:T(8,128)(2,1)} %own.1, bf16[3,512,512]{2,1,0:T(8,128)(2,1)} %cross.1, s32[3,512]{1,0:T(4,128)} %perm.1), custom_call_target="tpu_custom_call" | custom-call | flops 3221225472 | bytes 4194304 | tf_op jit(solution)/shard_map/pallas_call | solution.py:133
  36.9 0.8 %copy.6 = bf16[512,512]{1,0:T(8,128)(2,1)} copy(bf16[512,512]{1,0:T(8,128)(2,1)S(1)} %shard_map.46) | data formatting | bytes 1048576

commit v5 on v4

--- a/solution.py
+++ b/solution.py
@@ -10,7 +10,8 @@
 LEVELS = 3
 BODY = 32
 TAIL = (16, 16)
-AHEAD = 4
+FIRST = 6
+AHEAD = 3
 LAG = 32
 
 
@@ -84,7 +85,7 @@
         )
 
     copies = {}
-    for k in range(min(AHEAD, len(chunks))):
+    for k in range(min(FIRST, len(chunks))):
         copies[0, k] = send(0, k)
         copies[0, k].start()
 
@@ -110,16 +111,18 @@
             panels[level, rows] = result
             copies[level + 1, k] = send(level + 1, k)
             copies[level + 1, k].start()
-        if level == 0 and k + AHEAD < len(chunks):
+        else:
+            out[rows] = result
+        if level == 0 and FIRST <= k + AHEAD < len(chunks):
+            copies[0, k].wait_send()
             copies[0, k + AHEAD] = send(0, k + AHEAD)
             copies[0, k + AHEAD].start()
-        else:
-            out[rows] = result
 
     for level, k in step_order(chunks):
         step(level, k)
-    for copy in copies.values():
-        copy.wait_send()
+    for (level, k), copy in copies.items():
+        if level > 0 or not FIRST <= k + AHEAD < len(chunks):
+            copy.wait_send()
 
 
 def per_device(n_row, n_col, probes, own_blocks, cross_blocks, level_perm):

time: 37.8 us -> 41.4 us (1.095)
  the two profiles are of different devices: /device:TPU:8 before, /device:TPU:0 now
where the time goes in v5:
time: 41.4 us; the launch traced here: 41.2 us
  Pallas kernels  40.4 us (98%)
  local copies, waits for them, and re-layouts  0.8 us (2%)
    pallas_call x1, Pallas kernels, per_device(): pl.pallas_call(functools.partial(kernel, n_row, n_col, chunks), out_shape...  40.4 us

profile of v5, /device:TPU:0, one launch (start us, length us, event | category | flops | bytes accessed | tf_op | source)
XLA Modules:
  0.0 41.2 jit_solution(14503714623471415846)
XLA Ops:
  0.0 40.4 %shard_map.46 = bf16[512,512]{1,0:T(8,128)(2,1)S(1)} custom-call(bf16[512,512]{1,0:T(8,128)(2,1)} %probes.1, bf16[3,512,512]{2,1,0:T(8,128)(2,1)} %own.1, bf16[3,512,512]{2,1,0:T(8,128)(2,1)} %cross.1, s32[3,512]{1,0:T(4,128)} %perm.1), custom_call_target="tpu_custom_call" | custom-call | flops 3221225472 | bytes 4194304 | tf_op jit(solution)/shard_map/pallas_call | solution.py:136
  40.4 0.8 %copy.6 = bf16[512,512]{1,0:T(8,128)(2,1)} copy(bf16[512,512]{1,0:T(8,128)(2,1)S(1)} %shard_map.46) | data formatting | bytes 1048576

commit v6 on v4

--- a/solution.py
+++ b/solution.py
@@ -8,10 +8,12 @@
 from jax.sharding import PartitionSpec as P
 
 LEVELS = 3
-BODY = 32
-TAIL = (16, 16)
-AHEAD = 4
-LAG = 32
+BODY = 64
+TAIL = (32, 32, 32, 16, 16)
+AHEAD = 3
+NEAR = 40
+FAR = 160
+JOIN = 128
 
 
 def row_chunks(rows):
@@ -29,13 +31,18 @@
 
 def step_order(chunks):
     rows = sum(chunks[-1])
-    steps = []
+    steps, group = [], []
     for k, chunk in enumerate(chunks):
         due = sum(chunk)
-        for level in range(LEVELS):
-            steps.append((due, level, k))
-            due += min((AHEAD - 1) * BODY, max(rows - due, 0)) + LAG
-    return [(level, k) for _, level, k in sorted(steps)]
+        for level in range(LEVELS - 1):
+            steps.append((due, level, (k,)))
+            due += max(NEAR, min(FAR, 3 * (rows - due) // 4))
+        group.append(k)
+        size = sum(chunks[j][1] for j in group)
+        if size >= JOIN or k >= len(chunks) - 3 or k == len(chunks) - 1:
+            steps.append((due, LEVELS - 1, tuple(group)))
+            group = []
+    return [(level, ks) for _, level, ks in sorted(steps)]
 
 
 def flip(index, distance):
@@ -98,26 +105,27 @@
             moved = jnp.dot(source[level], pick, preferred_element_type=jnp.float32)
             target[level] = moved.astype(jnp.bfloat16)
 
-    def step(level, k):
-        start, size = chunks[k]
-        rows = pl.ds(start, size)
+    def step(level, ks):
+        start, k = chunks[ks[0]][0], ks[-1]
+        rows = pl.ds(start, sum(chunks[k]) - start)
         held = mine[rows] if level == 0 else panels[level - 1, rows]
         total = jnp.dot(held, own_p[level], preferred_element_type=jnp.float32)
-        copies[level, k].wait_recv()
+        for j in ks:
+            copies[level, j].wait_recv()
         total += jnp.dot(others[level, rows], cross_p[level], preferred_element_type=jnp.float32)
         result = total.astype(jnp.bfloat16)
-        if level < LEVELS - 1:
-            panels[level, rows] = result
-            copies[level + 1, k] = send(level + 1, k)
-            copies[level + 1, k].start()
+        if level == LEVELS - 1:
+            out[rows] = result
+            return
+        panels[level, rows] = result
+        copies[level + 1, k] = send(level + 1, k)
+        copies[level + 1, k].start()
         if level == 0 and k + AHEAD < len(chunks):
             copies[0, k + AHEAD] = send(0, k + AHEAD)
             copies[0, k + AHEAD].start()
-        else:
-            out[rows] = result
 
-    for level, k in step_order(chunks):
-        step(level, k)
+    for level, ks in step_order(chunks):
+        step(level, ks)
     for copy in copies.values():
         copy.wait_send()
 

time: 37.8 us -> 38.6 us (1.021)
  the two profiles are of different devices: /device:TPU:8 before, /device:TPU:0 now
where the time goes in v6:
time: 38.6 us; the launch traced here: 38.4 us
  Pallas kernels  37.6 us (97%)
  local copies, waits for them, and re-layouts  0.8 us (2%)
    pallas_call x1, Pallas kernels, per_device(): pl.pallas_call(functools.partial(kernel, n_row, n_col, chunks), out_shape...  37.6 us
    unnamed x1, local copies, waits for them, and re-layouts  0.8 us

profile of v6, /device:TPU:0, one launch (start us, length us, event | category | flops | bytes accessed | tf_op | source)
XLA Modules:
  0.0 38.4 jit_solution(5123656453480271495)
XLA Ops:
  0.0 37.6 %shard_map.46 = bf16[512,512]{1,0:T(8,128)(2,1)S(1)} custom-call(bf16[512,512]{1,0:T(8,128)(2,1)} %probes.1, bf16[3,512,512]{2,1,0:T(8,128)(2,1)} %own.1, bf16[3,512,512]{2,1,0:T(8,128)(2,1)} %cross.1, s32[3,512]{1,0:T(4,128)} %perm.1), custom_call_target="tpu_custom_call" | custom-call | flops 3221225472 | bytes 4194304 | tf_op jit(solution)/shard_map/pallas_call | solution.py:141
  37.6 0.8 %copy.6 = bf16[512,512]{1,0:T(8,128)(2,1)} copy(bf16[512,512]{1,0:T(8,128)(2,1)S(1)} %shard_map.46) | data formatting | bytes 1048576

commit v7 on v6

--- a/solution.py
+++ b/solution.py
@@ -9,10 +9,10 @@
 
 LEVELS = 3
 BODY = 64
-TAIL = (32, 32, 32, 16, 16)
+TAIL = (48, 32, 32, 16)
 AHEAD = 3
-NEAR = 40
-FAR = 160
+NEAR = 48
+FAR = 112
 JOIN = 128
 
 
@@ -38,8 +38,7 @@
             steps.append((due, level, (k,)))
             due += max(NEAR, min(FAR, 3 * (rows - due) // 4))
         group.append(k)
-        size = sum(chunks[j][1] for j in group)
-        if size >= JOIN or k >= len(chunks) - 3 or k == len(chunks) - 1:
+        if sum(chunks[j][1] for j in group) >= JOIN or len(chunks) - k in (1, 3):
             steps.append((due, LEVELS - 1, tuple(group)))
             group = []
     return [(level, ks) for _, level, ks in sorted(steps)]
@@ -53,7 +52,7 @@
     n_row, n_col, chunks,
     probes, own, cross, perm,
     out,
-    mine, own_v, cross_v, perm_v, own_p, cross_p, panels, others,
+    mine, own_v, cross_v, perm_v, own_p, cross_p, panels, others, base,
     load_sem, perm_sem, send_sem, recv_sem,
 ):
     row, col = lax.axis_index("row"), lax.axis_index("col")
@@ -105,11 +104,15 @@
             moved = jnp.dot(source[level], pick, preferred_element_type=jnp.float32)
             target[level] = moved.astype(jnp.bfloat16)
 
+    base[...] = jnp.dot(mine[...], own_p[0], preferred_element_type=jnp.float32)
+
     def step(level, ks):
         start, k = chunks[ks[0]][0], ks[-1]
         rows = pl.ds(start, sum(chunks[k]) - start)
-        held = mine[rows] if level == 0 else panels[level - 1, rows]
-        total = jnp.dot(held, own_p[level], preferred_element_type=jnp.float32)
+        if level == 0:
+            total = base[rows]
+        else:
+            total = jnp.dot(panels[level - 1, rows], own_p[level], preferred_element_type=jnp.float32)
         for j in ks:
             copies[level, j].wait_recv()
         total += jnp.dot(others[level, rows], cross_p[level], preferred_element_type=jnp.float32)
@@ -152,6 +155,7 @@
             weights,
             pltpu.VMEM((LEVELS - 1, rows, depth), jnp.bfloat16),
             pltpu.VMEM((LEVELS, rows, depth), jnp.bfloat16),
+            pltpu.VMEM((rows, depth), jnp.float32),
             pltpu.SemaphoreType.DMA((3,)),
             pltpu.SemaphoreType.DMA,
             pltpu.SemaphoreType.DMA((LEVELS, len(chunks))),

time: 38.6 us -> 38.7 us (level)
  no operation moved by 1% of the time
where the time goes in v7:
time: 38.7 us; the launch traced here: 38.5 us
  Pallas kernels  37.7 us (97%)
  local copies, waits for them, and re-layouts  0.8 us (2%)
    pallas_call x1, Pallas kernels, per_device(): pl.pallas_call(functools.partial(kernel, n_row, n_col, chunks), out_shape...  37.7 us
    unnamed x1, local copies, waits for them, and re-layouts  0.8 us

profile of v7, /device:TPU:0, one launch (start us, length us, event | category | flops | bytes accessed | tf_op | source)
XLA Modules:
  0.0 38.5 jit_solution(15480832282599619046)
XLA Ops:
  0.0 37.7 %shard_map.46 = bf16[512,512]{1,0:T(8,128)(2,1)S(1)} custom-call(bf16[512,512]{1,0:T(8,128)(2,1)} %probes.1, bf16[3,512,512]{2,1,0:T(8,128)(2,1)} %own.1, bf16[3,512,512]{2,1,0:T(8,128)(2,1)} %cross.1, s32[3,512]{1,0:T(4,128)} %perm.1), custom_call_target="tpu_custom_call" | custom-call | flops 3221225472 | bytes 4194304 | tf_op jit(solution)/shard_map/pallas_call | solution.py:144
  37.7 0.8 %copy.6 = bf16[512,512]{1,0:T(8,128)(2,1)} copy(bf16[512,512]{1,0:T(8,128)(2,1)S(1)} %shard_map.46) | data formatting | bytes 1048576

commit v8 on v7

--- a/solution.py
+++ b/solution.py
@@ -8,12 +8,12 @@
 from jax.sharding import PartitionSpec as P
 
 LEVELS = 3
-BODY = 64
-TAIL = (48, 32, 32, 16)
-AHEAD = 3
-NEAR = 48
-FAR = 112
-JOIN = 128
+BODY = 32
+TAIL = (16, 16)
+AHEAD = (6, 4)
+LAG = 32
+QUEUE = 96
+JOIN = 64
 
 
 def row_chunks(rows):
@@ -36,7 +36,7 @@
         due = sum(chunk)
         for level in range(LEVELS - 1):
             steps.append((due, level, (k,)))
-            due += max(NEAR, min(FAR, 3 * (rows - due) // 4))
+            due += min(QUEUE, max(rows - due, 0)) + LAG
         group.append(k)
         if sum(chunks[j][1] for j in group) >= JOIN or len(chunks) - k in (1, 3):
             steps.append((due, LEVELS - 1, tuple(group)))
@@ -90,9 +90,13 @@
         )
 
     copies = {}
-    for k in range(min(AHEAD, len(chunks))):
+    core = lax.rem(row, 2)
+    for k in range(len(chunks)):
         copies[0, k] = send(0, k)
-        copies[0, k].start()
+        if k < min(AHEAD):
+            copies[0, k].start()
+        elif k < max(AHEAD):
+            pl.when(core == AHEAD.index(max(AHEAD)))(copies[0, k].start)
 
     for load in loads:
         load.wait()
@@ -123,9 +127,10 @@
         panels[level, rows] = result
         copies[level + 1, k] = send(level + 1, k)
         copies[level + 1, k].start()
-        if level == 0 and k + AHEAD < len(chunks):
-            copies[0, k + AHEAD] = send(0, k + AHEAD)
-            copies[0, k + AHEAD].start()
+        if level == 0:
+            for which, ahead in enumerate(AHEAD):
+                if k + ahead < len(chunks):
+                    pl.when(core == which)(copies[0, k + ahead].start)
 
     for level, ks in step_order(chunks):
         step(level, ks)

time: 38.7 us -> 36.9 us (0.953); the launches traced: 38.5 us -> 36.2 us
  Pallas kernels: 37.7 us -> 35.4 us
    pallas_call x1, Pallas kernels: 37.7 us -> 35.4 us  [per_device(): pl.pallas_call(functools.partial(kernel, n_row, n_col, chunks), out_shape...]
where the time goes in v8:
time: 36.9 us; the launch traced here: 36.2 us
  Pallas kernels  35.4 us (96%)
  local copies, waits for them, and re-layouts  0.8 us (2%)
    pallas_call x1, Pallas kernels, per_device(): pl.pallas_call(functools.partial(kernel, n_row, n_col, chunks), out_shape...  35.4 us
    unnamed x1, local copies, waits for them, and re-layouts  0.8 us

profile of v8, /device:TPU:0, one launch (start us, length us, event | category | flops | bytes accessed | tf_op | source)
XLA Modules:
  0.0 36.2 jit_solution(12691697769632522774)
XLA Ops:
  0.0 35.4 %shard_map.46 = bf16[512,512]{1,0:T(8,128)(2,1)S(1)} custom-call(bf16[512,512]{1,0:T(8,128)(2,1)} %probes.1, bf16[3,512,512]{2,1,0:T(8,128)(2,1)} %own.1, bf16[3,512,512]{2,1,0:T(8,128)(2,1)} %cross.1, s32[3,512]{1,0:T(4,128)} %perm.1), custom_call_target="tpu_custom_call" | custom-call | flops 3221225472 | bytes 4194304 | tf_op jit(solution)/shard_map/pallas_call | solution.py:149
  35.4 0.8 %copy.6 = bf16[512,512]{1,0:T(8,128)(2,1)} copy(bf16[512,512]{1,0:T(8,128)(2,1)S(1)} %shard_map.46) | data formatting | bytes 1048576

commit v9 on v8

--- a/solution.py
+++ b/solution.py
@@ -10,7 +10,7 @@
 LEVELS = 3
 BODY = 32
 TAIL = (16, 16)
-AHEAD = (6, 4)
+AHEAD = (6, 4, 8, 6)
 LAG = 32
 QUEUE = 96
 JOIN = 64
@@ -90,13 +90,15 @@
         )
 
     copies = {}
-    core = lax.rem(row, 2)
+    place = 2 * lax.rem(lax.div(col, 2), 2) + lax.rem(row, 2)
     for k in range(len(chunks)):
         copies[0, k] = send(0, k)
         if k < min(AHEAD):
             copies[0, k].start()
-        elif k < max(AHEAD):
-            pl.when(core == AHEAD.index(max(AHEAD)))(copies[0, k].start)
+            continue
+        for which, ahead in enumerate(AHEAD):
+            if k < ahead:
+                pl.when(place == which)(copies[0, k].start)
 
     for load in loads:
         load.wait()
@@ -130,7 +132,7 @@
         if level == 0:
             for which, ahead in enumerate(AHEAD):
                 if k + ahead < len(chunks):
-                    pl.when(core == which)(copies[0, k + ahead].start)
+                    pl.when(place == which)(copies[0, k + ahead].start)
 
     for level, ks in step_order(chunks):
         step(level, ks)

time: 36.9 us -> 39.1 us (1.060); the launches traced: 36.2 us -> 38.9 us
  Pallas kernels: 35.4 us -> 38.1 us
    pallas_call x1, Pallas kernels: 35.4 us -> 38.1 us  [per_device(): pl.pallas_call(functools.partial(kernel, n_row, n_col, chunks), out_shape...]
where the time goes in v9:
time: 39.1 us; the launch traced here: 38.9 us
  Pallas kernels  38.1 us (97%)
  local copies, waits for them, and re-layouts  0.8 us (2%)
    pallas_call x1, Pallas kernels, per_device(): pl.pallas_call(functools.partial(kernel, n_row, n_col, chunks), out_shape...  38.1 us
    unnamed x1, local copies, waits for them, and re-layouts  0.8 us

profile of v9, /device:TPU:0, one launch (start us, length us, event | category | flops | bytes accessed | tf_op | source)
XLA Modules:
  0.0 38.9 jit_solution(17961984563046681862)
XLA Ops:
  0.0 38.1 %shard_map.46 = bf16[512,512]{1,0:T(8,128)(2,1)S(1)} custom-call(bf16[512,512]{1,0:T(8,128)(2,1)} %probes.1, bf16[3,512,512]{2,1,0:T(8,128)(2,1)} %own.1, bf16[3,512,512]{2,1,0:T(8,128)(2,1)} %cross.1, s32[3,512]{1,0:T(4,128)} %perm.1), custom_call_target="tpu_custom_call" | custom-call | flops 3221225472 | bytes 4194304 | tf_op jit(solution)/shard_map/pallas_call | solution.py:151
  38.1 0.8 %copy.6 = bf16[512,512]{1,0:T(8,128)(2,1)} copy(bf16[512,512]{1,0:T(8,128)(2,1)S(1)} %shard_map.46) | data formatting | bytes 1048576
